TPU v7x, 128 devices: a whole 4x4x4 slice. The times are simulated.
128 devices in a mesh: row: 8 (over z_hi, x), col: 16 (over z_lo, y, core).
Axes of the slice: x: 4, y: 4, z: 4 (z_hi: 2, z_lo: 2; z = z_hi * 2 + z_lo), core: 2. Of those that a mesh axis runs over, the one named last changes fastest.
Arguments:
- depth: float32 [2048, 16384], P('row', 'col'), may hold values from 0.05 to 3
- flow_east: float32 [2048, 16384], P('row', 'col'), may hold values from -3 to 3
- flow_south: float32 [2048, 16384], P('row', 'col'), may hold values from -3 to 3
- elevation: float32 [2048, 16384], P('row', 'col'), may hold values from -3 to 3
- roughness: float32 [2048, 16384], P('row', 'col'), may hold values from 0.02 to 0.15
- wet_mask: int32 [2048, 16384], P('row', 'col'), may hold values 0 or 1
- rainfall: bfloat16 [2, 3, 2048, 16384], P(None, None, ('row', 'col')), may hold values from 0.0019989014 to 0.049804688
- panel_source: int32 [256, 128], P('row', 'col'), may hold values from 0 to 2
- inflow: float32 [32768, 128], P(('row', 'col')), may hold values from 0.01 to 0.2
- gauge_tile: int32 [32768, 1], P(('row', 'col')), may hold values from 0 to 127; in each aligned block of 256 rows (0 to 255, 256 to 511, ...) at most 4 rows name the same one
- gauge_cell: int32 [32768], P(('row', 'col')), may hold values from 0 to 2047
Outputs:
- depth_out: float32 [2048, 16384], P('row', 'col')
- east_out: float32 [2048, 16384], P('row', 'col')
- south_out: float32 [2048, 16384], P('row', 'col')
Inputs may be any that keep to these rules, and one draw needn't show every extreme that they name: `gauge_tile`: among the gauges of one device no tile is named more than 4 times, a bound that some block reaches.
All inputs are finite; a program needn't handle non-finite values. No bound on the sum of `wet_mask` on one device may be relied on, other than what follows from the above.
Results may differ from a plain program's by a relative error of at most 0.0003.
Values may be sent and summed in bfloat16 or wider, within the bound.
A program may use at most 192 MiB of HBM per device.

v0:
```python
import jax
import jax.numpy as jnp
from jax import lax
from jax.sharding import PartitionSpec as P

STEPS = 20
FRAMES = 2
PANEL_ROWS = 8
BLOCK = 128
CAP = 4


gravity = 9.81
time_step = 5.0
cell_size = 90.0
depth_floor = 0.1


def from_behind(value, axis, steps):
    count = lax.axis_size(axis)
    leading, last = (max(0, -steps), min(count, count - steps))
    return lax.ppermute(value, axis, [(source, source + steps) for source in range(leading, last)])


def select_source(rain, source_map):
    frames, sources, rows, cols = rain.shape
    shaped = rain.reshape(frames, sources, rows // PANEL_ROWS, PANEL_ROWS, cols // BLOCK, BLOCK)
    picker = source_map[:, None, :, None]
    chosen = shaped[:, 0]
    for source in range(1, sources):
        chosen = jnp.where(picker == source, shaped[:, source], chosen)
    return chosen.reshape(frames, rows, cols)


def face_flow(flow, eta, eta_next, zmax, fric, opened):
    depth_face = jnp.maximum(jnp.maximum(eta, eta_next) - zmax, depth_floor)
    slope = (eta_next - eta) / cell_size
    driven = flow - gravity * depth_face * time_step * slope
    return opened * driven / (1.0 + fric * jnp.abs(flow) / jnp.power(depth_face, 7.0 / 3.0))


def body(
    depth,
    flow_east,
    flow_south,
    elevation,
    roughness,
    wet_mask,
    rainfall,
    panel_source,
    inflow,
    gauge_tile,
    gauge_cell,
):
    tile_rows, tile_cols = depth.shape
    n_row = lax.axis_size("row")
    n_col = lax.axis_size("col")
    devices = n_row * n_col
    moved = lax.all_to_all(rainfall, "col", split_axis=3, concat_axis=2, tiled=True)
    rain_tile = select_source(moved, panel_source)
    target = gauge_tile[:, 0]
    onehot = (target[:, None] == jnp.arange(devices, dtype=jnp.int32)[None, :]).astype(jnp.float32)
    earlier = jnp.cumsum(onehot, axis=0) - onehot
    rank = jnp.sum(earlier * onehot, axis=1).astype(jnp.int32)
    slot = target * CAP + rank
    send_vals = jnp.zeros((devices * CAP, BLOCK), jnp.float32).at[slot].set(inflow)
    send_cells = (
        jnp.zeros((devices * CAP,), jnp.float32).at[slot].set(gauge_cell.astype(jnp.float32))
    )
    got_vals, got_cells = (
        lax.all_to_all(
            send_vals.reshape(devices, CAP, BLOCK),
            ("row", "col"),
            split_axis=0,
            concat_axis=0,
            tiled=True,
        ),
        lax.all_to_all(
            send_cells.reshape(devices, CAP),
            ("row", "col"),
            split_axis=0,
            concat_axis=0,
            tiled=True,
        ),
    )
    positions = got_cells.reshape(-1).astype(jnp.int32)
    source_in = (
        jnp.zeros((tile_rows * (tile_cols // BLOCK), BLOCK), jnp.float32)
        .at[positions]
        .add(got_vals.reshape(-1, BLOCK))
        .reshape(tile_rows, tile_cols)
    )
    maskf = wet_mask.astype(jnp.float32)
    ratio = time_step / cell_size
    east_edge = from_behind(jnp.stack([elevation[:, 0], roughness[:, 0], maskf[:, 0]]), "col", -1)
    south_edge = from_behind(jnp.stack([elevation[0, :], roughness[0, :], maskf[0, :]]), "row", -1)
    elev_e = jnp.concatenate([elevation[:, 1:], east_edge[0][:, None]], 1)
    rough_e = jnp.concatenate([roughness[:, 1:], east_edge[1][:, None]], 1)
    mask_e = jnp.concatenate([maskf[:, 1:], east_edge[2][:, None]], 1)
    elev_s = jnp.concatenate([elevation[1:, :], south_edge[0][None, :]], 0)
    rough_s = jnp.concatenate([roughness[1:, :], south_edge[1][None, :]], 0)
    mask_s = jnp.concatenate([maskf[1:, :], south_edge[2][None, :]], 0)
    open_e = maskf * mask_e
    open_s = maskf * mask_s
    zmax_e = jnp.maximum(elevation, elev_e)
    zmax_s = jnp.maximum(elevation, elev_s)
    fric_e = gravity * time_step * jnp.square(0.5 * (roughness + rough_e))
    fric_s = gravity * time_step * jnp.square(0.5 * (roughness + rough_s))

    def advance(step, state):
        height, east_q, south_q = state
        eta = height + elevation
        depth_e = from_behind(height[:, 0], "col", -1)
        depth_s = from_behind(height[0, :], "row", -1)
        eta_e = jnp.concatenate([eta[:, 1:], (depth_e + east_edge[0])[:, None]], 1)
        eta_s = jnp.concatenate([eta[1:, :], (depth_s + south_edge[0])[None, :]], 0)
        east_q = face_flow(east_q, eta, eta_e, zmax_e, fric_e, open_e)
        south_q = face_flow(south_q, eta, eta_s, zmax_s, fric_s, open_s)
        west_edge = from_behind(east_q[:, -1], "col", 1)
        north_edge = from_behind(south_q[-1, :], "row", 1)
        west_q = jnp.concatenate([west_edge[:, None], east_q[:, :-1]], 1)
        north_q = jnp.concatenate([north_edge[None, :], south_q[:-1, :]], 0)
        frame = step * FRAMES // STEPS
        rain_now = lax.dynamic_index_in_dim(rain_tile, frame, 0, keepdims=False)
        height = (
            height
            + ratio * (west_q - east_q + (north_q - south_q))
            + (rain_now.astype(jnp.float32) + source_in)
        )
        return (height, east_q, south_q)

    height, east_q, south_q = lax.fori_loop(0, STEPS, advance, (depth, flow_east, flow_south))
    return (height, east_q, south_q)


def solution(mesh):
    placed = (
        P("row", "col"),
        P("row", "col"),
        P("row", "col"),
        P("row", "col"),
        P("row", "col"),
        P("row", "col"),
        P(None, None, ("row", "col"), None),
        P("row", "col"),
        P(("row", "col"), None),
        P(("row", "col"), None),
        P(("row", "col")),
    )
    return jax.shard_map(
        body,
        mesh=mesh,
        in_specs=placed,
        out_specs=(P("row", "col"), P("row", "col"), P("row", "col")),
        check_vma=False,
    )
```

profile of v0, /device:TPU:38, one launch (start us, length us, event | category | flops | bytes accessed | tf_op | source)
XLA Modules:
  0.0 933.0 jit_solution(14582281648070290550)
XLA Ops:
  5.8 10.2 %all-to-all-start.1 = ((f32[128,1,4]{2,1,0:T(1,128)}), f32[128,1,4]{2,1,0:T(1,128)S(1)}, u32[]{:S(2)}, u32[]{:S(2)}) async-start(f32[128,1,4]{2,1,0:T(1,128)} %bitcast.22), calls=%async_computation.1 | async-start | bytes 131072 | tf_op jit(solution)/shard_map/all_to_all | solution.py:78
  23.5 6.4 all-to-all-start.2
  30.1 36.7 %copy.58 = bf16[2,3,16,16384]{2,1,0,3:T(4,128)(2,1)} copy(bf16[2,3,16,16384]{3,2,1,0:T(8,128)(2,1)} %param.19) | data formatting | bytes 6291456 | tf_op args[6]
  66.7 29.5 %reshape.131 = bf16[16,2,49152]{2,1,0:T(2,128)(2,1)} reshape(bf16[16384,2,3,16]{3,2,1,0:T(4,128)(2,1)} %bitcast.93) | data formatting | bytes 6291456
  96.9 6.0 all-to-all-start
  120.6 17.3 %collective-permute-done.4 = f32[3,256]{1,0:T(4,128)S(1)} collective-permute-done((f32[3,256]{1,0:T(4,128)S(1)}, f32[3,256]{1,0:T(4,128)S(1)}, u32[]{:S(2)}, u32[]{:S(2)}) %collective-permute-start.4) | collective-permute-done | bytes 3104 | tf_op jit(solution)/shard_map/ppermute | solution.py:22
  151.2 33.5 %reshape.132 = bf16[16384,2,3,16]{3,2,1,0:T(4,128)(2,1)} reshape(bf16[16,2,49152]{2,1,0:T(2,128)(2,1)} %all-to-all-done) | data formatting | bytes 6291456
  184.7 43.0 %copy.59 = bf16[2,3,16,16,1024]{4,2,3,1,0:T(8,128)(2,1)} copy(bf16[2,3,16,16,1024]{2,1,0,4,3:T(4,128)(2,1)} %bitcast.92) | data formatting | bytes 6291456 | tf_op jit(solution)/shard_map/all_to_all | solution.py:59
  240.4 691.2 %while.20 = (s32[]{:T(128)}, f32[256,1024]{1,0:T(8,128)}, f32[256,1024]{1,0:T(8,128)S(1)}, f32[256,1024]{1,0:T(8,128)S(1)}, f32[256,1024]{1,0:T(8,128)S(1)}, /*i...) while((s32[]{:T(128)}, f32[256,1024]{1,0:T(8,128)}, ...), condition=%wide.region_7.8_spmd, body=%wide.region_6.7_spmd.sunk | while | flops 10749198 | bytes 33111540 | solution.py:132
  245.0 5.7 collective-permute-start.1
  255.7 5.4 add_divide_fusion.3
  261.1 6.1 collective-permute-start.3
  295.5 6.7 collective-permute-start.3
  329.0 7.5 collective-permute-start.3
  357.9 5.4 add_divide_fusion.3
  363.4 7.5 collective-permute-start.3
  397.7 7.5 collective-permute-start.3
  432.1 7.5 collective-permute-start.3
  466.5 7.5 collective-permute-start.3
  500.9 7.5 collective-permute-start.3
  535.2 7.5 collective-permute-start.3
  569.6 7.5 collective-permute-start.3
  604.0 7.5 collective-permute-start.3
  638.3 7.5 collective-permute-start.3
  672.7 7.5 collective-permute-start.3
  707.1 7.5 collective-permute-start.3
  741.5 7.5 collective-permute-start.3
  775.8 7.5 collective-permute-start.3
  810.2 7.5 collective-permute-start.3
  844.6 7.5 collective-permute-start.3
  879.0 7.5 collective-permute-start.3
  913.3 7.5 collective-permute-start.3
  (574 shorter events, 581.8 us)
Async XLA Ops:
  5.8 17.8 %all-to-all-start.1 = ((f32[128,1,4]{2,1,0:T(1,128)}), f32[128,1,4]{2,1,0:T(1,128)S(1)}, u32[]{:S(2)}, u32[]{:S(2)}) async-start(f32[128,1,4]{2,1,0:T(1,128)} %bitcast.22), calls=%async_computation.1 | async-start | bytes 131072 | tf_op jit(solution)/shard_map/all_to_all | solution.py:78
  23.5 72.7 %all-to-all-start.2 = ((f32[128,4,128]{2,1,0:T(4,128)}), f32[128,4,128]{2,1,0:T(4,128)S(1)}, u32[]{:S(2)}, u32[]{:S(2)}) async-start(f32[128,4,128]{2,1,0:T(4,128)} %bitcast.24), calls=%async_computation.2 | async-start | bytes 524288 | tf_op jit(solution)/shard_map/all_to_all | solution.py:71
  96.9 54.3 %all-to-all-start = ((bf16[16,2,49152]{2,1,0:T(2,128)(2,1)}), bf16[16,2,49152]{2,1,0:T(2,128)(2,1)}, u32[]{:S(2)}, u32[]{:S(2)}) async-start(bf16[16,2,49152]{2,1,0:T(2,128)(2,1)} %reshape.131), calls=%async_computation | async-start | bytes 6291456 | tf_op jit(solution)/shard_map/all_to_all | solution.py:59
  103.3 34.6 %collective-permute-start.4 = (f32[3,256]{1,0:T(4,128)S(1)}, f32[3,256]{1,0:T(4,128)S(1)}, u32[]{:S(2)}, u32[]{:S(2)}) collective-permute-start(f32[3,256]{1,0:T(4,128)S(1)} %pad_maximum_fusion.3), channel_id=1, source_target_pairs={{1,0},{2,1},{3,2},{4,3},{5,4},{6,5},{7,6},{8,7},{9,8},{10,9},{11,1... | collective-permute-start | bytes 9224 | tf_op jit(solution)/shard_map/ppermute | solution.py:22
  108.3 31.4 %collective-permute-start.5 = (f32[3,1024]{1,0:T(4,128)}, f32[3,1024]{1,0:T(4,128)}, u32[]{:S(2)}, u32[]{:S(2)}) collective-permute-start(f32[3,1024]{1,0:T(4,128)} %pad_maximum_fusion.2), channel_id=1, source_target_pairs={{16,0},{32,16},{48,32},{64,48},{80,64},{96,80},{112,96},{17,1},{33... | collective-permute-start | bytes 36872 | tf_op jit(solution)/shard_map/ppermute | solution.py:22
  241.2 14.4 %collective-permute-start = (f32[1024]{0:T(1024)S(1)}, f32[1024]{0:T(1024)S(1)}, u32[]{:S(2)}, u32[]{:S(2)}) collective-permute-start(f32[1024]{0:T(1024)S(1)} %bitcast.105), channel_id=1, source_target_pairs={{16,0},{32,16},{48,32},{64,48},{80,64},{96,80},{112,96},{17,1},{33... | collective-permute-start | bytes 12296 | tf_op jit(solution)/shard_map/while/body/eval_jaxpr/ppermute | solution.py:22
  245.0 10.5 %collective-permute-start.1 = (f32[256]{0:T(256)S(1)}, f32[256]{0:T(256)S(1)}, u32[]{:S(2)}, u32[]{:S(2)}) collective-permute-start(f32[256]{0:T(256)S(1)} %slice_reduce_fusion.7), channel_id=1, source_target_pairs={{1,0},{2,1},{3,2},{4,3},{5,4},{6,5},{7,6},{8,7},{9,8},{10,9},{11,1... | collective-permute-start | bytes 3080 | tf_op jit(solution)/shard_map/while/body/eval_jaxpr/ppermute | solution.py:22
  261.1 13.6 %collective-permute-start.3 = (f32[1024]{0:T(1024)S(1)}, f32[1024]{0:T(1024)S(1)}, u32[]{:S(2)}, u32[]{:S(2)}) collective-permute-start(f32[1024]{0:T(1024)S(1)} %bitcast.104), channel_id=1, source_target_pairs={{0,16},{16,32},{32,48},{48,64},{64,80},{80,96},{96,112},{1,17},{17... | collective-permute-start | bytes 12296 | tf_op jit(solution)/shard_map/while/body/eval_jaxpr/ppermute | solution.py:22
  278.9 11.1 %collective-permute-start = (f32[1024]{0:T(1024)S(1)}, f32[1024]{0:T(1024)S(1)}, u32[]{:S(2)}, u32[]{:S(2)}) collective-permute-start(f32[1024]{0:T(1024)S(1)} %bitcast.105), channel_id=1, source_target_pairs={{16,0},{32,16},{48,32},{64,48},{80,64},{96,80},{112,96},{17,1},{33... | collective-permute-start | bytes 12296 | tf_op jit(solution)/shard_map/while/body/eval_jaxpr/ppermute | solution.py:22
  295.5 14.0 %collective-permute-start.3 = (f32[1024]{0:T(1024)S(1)}, f32[1024]{0:T(1024)S(1)}, u32[]{:S(2)}, u32[]{:S(2)}) collective-permute-start(f32[1024]{0:T(1024)S(1)} %bitcast.104), channel_id=1, source_target_pairs={{0,16},{16,32},{32,48},{48,64},{64,80},{80,96},{96,112},{1,17},{17... | collective-permute-start | bytes 12296 | tf_op jit(solution)/shard_map/while/body/eval_jaxpr/ppermute | solution.py:22
  313.7 9.8 %collective-permute-start = (f32[1024]{0:T(1024)S(1)}, f32[1024]{0:T(1024)S(1)}, u32[]{:S(2)}, u32[]{:S(2)}) collective-permute-start(f32[1024]{0:T(1024)S(1)} %bitcast.105), channel_id=1, source_target_pairs={{16,0},{32,16},{48,32},{64,48},{80,64},{96,80},{112,96},{17,1},{33... | collective-permute-start | bytes 12296 | tf_op jit(solution)/shard_map/while/body/eval_jaxpr/ppermute | solution.py:22
  329.0 14.9 %collective-permute-start.3 = (f32[1024]{0:T(1024)S(1)}, f32[1024]{0:T(1024)S(1)}, u32[]{:S(2)}, u32[]{:S(2)}) collective-permute-start(f32[1024]{0:T(1024)S(1)} %bitcast.104), channel_id=1, source_target_pairs={{0,16},{16,32},{32,48},{48,64},{64,80},{80,96},{96,112},{1,17},{17... | collective-permute-start | bytes 12296 | tf_op jit(solution)/shard_map/while/body/eval_jaxpr/ppermute | solution.py:22
  363.4 14.9 %collective-permute-start.3 = (f32[1024]{0:T(1024)S(1)}, f32[1024]{0:T(1024)S(1)}, u32[]{:S(2)}, u32[]{:S(2)}) collective-permute-start(f32[1024]{0:T(1024)S(1)} %bitcast.104), channel_id=1, source_target_pairs={{0,16},{16,32},{32,48},{48,64},{64,80},{80,96},{96,112},{1,17},{17... | collective-permute-start | bytes 12296 | tf_op jit(solution)/shard_map/while/body/eval_jaxpr/ppermute | solution.py:22
  397.7 14.9 %collective-permute-start.3 = (f32[1024]{0:T(1024)S(1)}, f32[1024]{0:T(1024)S(1)}, u32[]{:S(2)}, u32[]{:S(2)}) collective-permute-start(f32[1024]{0:T(1024)S(1)} %bitcast.104), channel_id=1, source_target_pairs={{0,16},{16,32},{32,48},{48,64},{64,80},{80,96},{96,112},{1,17},{17... | collective-permute-start | bytes 12296 | tf_op jit(solution)/shard_map/while/body/eval_jaxpr/ppermute | solution.py:22
  432.1 14.9 %collective-permute-start.3 = (f32[1024]{0:T(1024)S(1)}, f32[1024]{0:T(1024)S(1)}, u32[]{:S(2)}, u32[]{:S(2)}) collective-permute-start(f32[1024]{0:T(1024)S(1)} %bitcast.104), channel_id=1, source_target_pairs={{0,16},{16,32},{32,48},{48,64},{64,80},{80,96},{96,112},{1,17},{17... | collective-permute-start | bytes 12296 | tf_op jit(solution)/shard_map/while/body/eval_jaxpr/ppermute | solution.py:22
  466.5 14.9 %collective-permute-start.3 = (f32[1024]{0:T(1024)S(1)}, f32[1024]{0:T(1024)S(1)}, u32[]{:S(2)}, u32[]{:S(2)}) collective-permute-start(f32[1024]{0:T(1024)S(1)} %bitcast.104), channel_id=1, source_target_pairs={{0,16},{16,32},{32,48},{48,64},{64,80},{80,96},{96,112},{1,17},{17... | collective-permute-start | bytes 12296 | tf_op jit(solution)/shard_map/while/body/eval_jaxpr/ppermute | solution.py:22
  500.9 14.9 %collective-permute-start.3 = (f32[1024]{0:T(1024)S(1)}, f32[1024]{0:T(1024)S(1)}, u32[]{:S(2)}, u32[]{:S(2)}) collective-permute-start(f32[1024]{0:T(1024)S(1)} %bitcast.104), channel_id=1, source_target_pairs={{0,16},{16,32},{32,48},{48,64},{64,80},{80,96},{96,112},{1,17},{17... | collective-permute-start | bytes 12296 | tf_op jit(solution)/shard_map/while/body/eval_jaxpr/ppermute | solution.py:22
  535.2 14.9 %collective-permute-start.3 = (f32[1024]{0:T(1024)S(1)}, f32[1024]{0:T(1024)S(1)}, u32[]{:S(2)}, u32[]{:S(2)}) collective-permute-start(f32[1024]{0:T(1024)S(1)} %bitcast.104), channel_id=1, source_target_pairs={{0,16},{16,32},{32,48},{48,64},{64,80},{80,96},{96,112},{1,17},{17... | collective-permute-start | bytes 12296 | tf_op jit(solution)/shard_map/while/body/eval_jaxpr/ppermute | solution.py:22
  554.3 9.8 %collective-permute-start = (f32[1024]{0:T(1024)S(1)}, f32[1024]{0:T(1024)S(1)}, u32[]{:S(2)}, u32[]{:S(2)}) collective-permute-start(f32[1024]{0:T(1024)S(1)} %bitcast.105), channel_id=1, source_target_pairs={{16,0},{32,16},{48,32},{64,48},{80,64},{96,80},{112,96},{17,1},{33... | collective-permute-start | bytes 12296 | tf_op jit(solution)/shard_map/while/body/eval_jaxpr/ppermute | solution.py:22
  569.6 14.9 %collective-permute-start.3 = (f32[1024]{0:T(1024)S(1)}, f32[1024]{0:T(1024)S(1)}, u32[]{:S(2)}, u32[]{:S(2)}) collective-permute-start(f32[1024]{0:T(1024)S(1)} %bitcast.104), channel_id=1, source_target_pairs={{0,16},{16,32},{32,48},{48,64},{64,80},{80,96},{96,112},{1,17},{17... | collective-permute-start | bytes 12296 | tf_op jit(solution)/shard_map/while/body/eval_jaxpr/ppermute | solution.py:22
  588.7 9.8 %collective-permute-start = (f32[1024]{0:T(1024)S(1)}, f32[1024]{0:T(1024)S(1)}, u32[]{:S(2)}, u32[]{:S(2)}) collective-permute-start(f32[1024]{0:T(1024)S(1)} %bitcast.105), channel_id=1, source_target_pairs={{16,0},{32,16},{48,32},{64,48},{80,64},{96,80},{112,96},{17,1},{33... | collective-permute-start | bytes 12296 | tf_op jit(solution)/shard_map/while/body/eval_jaxpr/ppermute | solution.py:22
  604.0 14.9 %collective-permute-start.3 = (f32[1024]{0:T(1024)S(1)}, f32[1024]{0:T(1024)S(1)}, u32[]{:S(2)}, u32[]{:S(2)}) collective-permute-start(f32[1024]{0:T(1024)S(1)} %bitcast.104), channel_id=1, source_target_pairs={{0,16},{16,32},{32,48},{48,64},{64,80},{80,96},{96,112},{1,17},{17... | collective-permute-start | bytes 12296 | tf_op jit(solution)/shard_map/while/body/eval_jaxpr/ppermute | solution.py:22
  623.0 9.8 %collective-permute-start = (f32[1024]{0:T(1024)S(1)}, f32[1024]{0:T(1024)S(1)}, u32[]{:S(2)}, u32[]{:S(2)}) collective-permute-start(f32[1024]{0:T(1024)S(1)} %bitcast.105), channel_id=1, source_target_pairs={{16,0},{32,16},{48,32},{64,48},{80,64},{96,80},{112,96},{17,1},{33... | collective-permute-start | bytes 12296 | tf_op jit(solution)/shard_map/while/body/eval_jaxpr/ppermute | solution.py:22
  638.3 14.9 %collective-permute-start.3 = (f32[1024]{0:T(1024)S(1)}, f32[1024]{0:T(1024)S(1)}, u32[]{:S(2)}, u32[]{:S(2)}) collective-permute-start(f32[1024]{0:T(1024)S(1)} %bitcast.104), channel_id=1, source_target_pairs={{0,16},{16,32},{32,48},{48,64},{64,80},{80,96},{96,112},{1,17},{17... | collective-permute-start | bytes 12296 | tf_op jit(solution)/shard_map/while/body/eval_jaxpr/ppermute | solution.py:22
  672.7 14.9 %collective-permute-start.3 = (f32[1024]{0:T(1024)S(1)}, f32[1024]{0:T(1024)S(1)}, u32[]{:S(2)}, u32[]{:S(2)}) collective-permute-start(f32[1024]{0:T(1024)S(1)} %bitcast.104), channel_id=1, source_target_pairs={{0,16},{16,32},{32,48},{48,64},{64,80},{80,96},{96,112},{1,17},{17... | collective-permute-start | bytes 12296 | tf_op jit(solution)/shard_map/while/body/eval_jaxpr/ppermute | solution.py:22
  707.1 14.9 %collective-permute-start.3 = (f32[1024]{0:T(1024)S(1)}, f32[1024]{0:T(1024)S(1)}, u32[]{:S(2)}, u32[]{:S(2)}) collective-permute-start(f32[1024]{0:T(1024)S(1)} %bitcast.104), channel_id=1, source_target_pairs={{0,16},{16,32},{32,48},{48,64},{64,80},{80,96},{96,112},{1,17},{17... | collective-permute-start | bytes 12296 | tf_op jit(solution)/shard_map/while/body/eval_jaxpr/ppermute | solution.py:22
  741.5 14.9 %collective-permute-start.3 = (f32[1024]{0:T(1024)S(1)}, f32[1024]{0:T(1024)S(1)}, u32[]{:S(2)}, u32[]{:S(2)}) collective-permute-start(f32[1024]{0:T(1024)S(1)} %bitcast.104), channel_id=1, source_target_pairs={{0,16},{16,32},{32,48},{48,64},{64,80},{80,96},{96,112},{1,17},{17... | collective-permute-start | bytes 12296 | tf_op jit(solution)/shard_map/while/body/eval_jaxpr/ppermute | solution.py:22
  775.8 14.9 %collective-permute-start.3 = (f32[1024]{0:T(1024)S(1)}, f32[1024]{0:T(1024)S(1)}, u32[]{:S(2)}, u32[]{:S(2)}) collective-permute-start(f32[1024]{0:T(1024)S(1)} %bitcast.104), channel_id=1, source_target_pairs={{0,16},{16,32},{32,48},{48,64},{64,80},{80,96},{96,112},{1,17},{17... | collective-permute-start | bytes 12296 | tf_op jit(solution)/shard_map/while/body/eval_jaxpr/ppermute | solution.py:22
  810.2 14.9 %collective-permute-start.3 = (f32[1024]{0:T(1024)S(1)}, f32[1024]{0:T(1024)S(1)}, u32[]{:S(2)}, u32[]{:S(2)}) collective-permute-start(f32[1024]{0:T(1024)S(1)} %bitcast.104), channel_id=1, source_target_pairs={{0,16},{16,32},{32,48},{48,64},{64,80},{80,96},{96,112},{1,17},{17... | collective-permute-start | bytes 12296 | tf_op jit(solution)/shard_map/while/body/eval_jaxpr/ppermute | solution.py:22
  844.6 14.9 %collective-permute-start.3 = (f32[1024]{0:T(1024)S(1)}, f32[1024]{0:T(1024)S(1)}, u32[]{:S(2)}, u32[]{:S(2)}) collective-permute-start(f32[1024]{0:T(1024)S(1)} %bitcast.104), channel_id=1, source_target_pairs={{0,16},{16,32},{32,48},{48,64},{64,80},{80,96},{96,112},{1,17},{17... | collective-permute-start | bytes 12296 | tf_op jit(solution)/shard_map/while/body/eval_jaxpr/ppermute | solution.py:22
  879.0 14.9 %collective-permute-start.3 = (f32[1024]{0:T(1024)S(1)}, f32[1024]{0:T(1024)S(1)}, u32[]{:S(2)}, u32[]{:S(2)}) collective-permute-start(f32[1024]{0:T(1024)S(1)} %bitcast.104), channel_id=1, source_target_pairs={{0,16},{16,32},{32,48},{48,64},{64,80},{80,96},{96,112},{1,17},{17... | collective-permute-start | bytes 12296 | tf_op jit(solution)/shard_map/while/body/eval_jaxpr/ppermute | solution.py:22
  913.3 14.9 %collective-permute-start.3 = (f32[1024]{0:T(1024)S(1)}, f32[1024]{0:T(1024)S(1)}, u32[]{:S(2)}, u32[]{:S(2)}) collective-permute-start(f32[1024]{0:T(1024)S(1)} %bitcast.104), channel_id=1, source_target_pairs={{0,16},{16,32},{32,48},{48,64},{64,80},{80,96},{96,112},{1,17},{17... | collective-permute-start | bytes 12296 | tf_op jit(solution)/shard_map/while/body/eval_jaxpr/ppermute | solution.py:22
  (92 other events, 611.4 us)
where the time goes:
time: 943 us; the launch traced here: 933 us
  starting transfers between devices  303 us (32%)
  local copies, waits for them, and re-layouts  281 us (30%)
  other arithmetic  225 us (24%)
  waiting for transfers between devices  120 us (13%)
    ppermute x82, starting transfers between devices, from_behind(): lax.ppermute(value, axis, [(source, source + steps) for source in range(l...  280 us
    ppermute x82, waiting for transfers between devices, from_behind(): lax.ppermute(value, axis, [(source, source + steps) for source in range(l...  115 us
    div x20, other arithmetic, face_flow(): opened * driven  108 us
    unnamed x42, local copies, waits for them, and re-layouts  107 us
    add x20, other arithmetic, advance(): height + ratio * (west_q - east_q + (north_q - south_q))  68.6 us
    all_to_all x1, local copies, waits for them, and re-layouts, body(): lax.all_to_all(rainfall, 'col', split_axis=3, concat_axis=2, tiled=True)  43 us
    slice x40, local copies, waits for them, and re-layouts, advance(): eta_s = jnp.concatenate([eta[1:, :], (depth_s + south_edge[0])[None, :]], 0)  35.6 us
    add x20, other arithmetic, advance(): eta = height + elevation  33.6 us
  transfers between devices with their start and end apart: 85, of which 22 were waited for; matrix products, arithmetic and copies ran while one was open for 23% of the time, Pallas kernels for 0%

commit v1 on v0

v1 whole, which is shorter than its diff:
```python
import functools

import jax
import jax.numpy as jnp
from jax import lax
from jax.experimental import pallas as pl
from jax.experimental.pallas import tpu as pltpu
from jax.sharding import PartitionSpec as P

STEPS = 20
FRAMES = 2
SOURCES = 3
PANEL_ROWS = 8
LANES = 128
CAP = 4
NR = 8
NCOL = 16
TR = 256
NB = 8
HALO = 24
BASE = 32
RP = 320
STRIPE = TR // NCOL
GD = 256
NX = 5

GRAVITY = 9.81
DT = 5.0
DX = 90.0
RATIO = DT / DX
SCALE = RATIO * GRAVITY * DT / DX
QSCALE = SCALE * RATIO
FLOOR = 0.1 * SCALE
FRIC = GRAVITY * DT * 0.25 * SCALE ** (7.0 / 3.0) / QSCALE
MESH = pl.DeviceIdType.MESH


def split3(x):
    hi = x.astype(jnp.bfloat16)
    rest = x - hi.astype(jnp.float32)
    mid = rest.astype(jnp.bfloat16)
    low = (rest - mid.astype(jnp.float32)).astype(jnp.bfloat16)
    return jnp.concatenate([hi, mid, low], axis=1)


def join3(x):
    return (x[:, :LANES] + x[:, LANES : 2 * LANES]) + x[:, 2 * LANES :]


def dot(a, b):
    return lax.dot_general(a, b, (((1,), (0,)), ((), ())), preferred_element_type=jnp.float32)


def iota(shape, axis):
    return lax.broadcasted_iota(jnp.int32, shape, axis)


def face(eta, nxt, q, zmax, fric, base):
    hf = jnp.maximum(jnp.maximum(eta, nxt) - zmax, FLOOR)
    drv = q - hf * (nxt - eta)
    pw = jnp.exp2(jnp.log2(hf) * (-7.0 / 3.0))
    return drv * (1.0 / (base + jnp.abs(q) * fric * pw))


def mul8(x):
    return pl.multiple_of(x * 8, 8)


def kernel(
    depth, flow_e, flow_s, elev, rough, wet, rain, panel, inflow, gtile, gcell,
    out_h, out_e, out_s,
    stage, wet_v, rain_v, panel_v, inflow_v, gtile_v, gcell_v,
    X, ZE, ZS, FE, FS, BE, BS, EN, S, SG,
    panel_r, ga, ga_r, gb, gb_r, rs, rx, pack_l, pack_r, got_l, got_r, spack_l, spack_r, sgot_l, sgot_r, outs,
    loc, panel_ss, panel_rs, ga_ss, ga_rs, gb_ss, gb_rs, rain_ss, rain_rs,
    col_ss, col_rs, row_ss, row_rs, row8_ss, row8_rs,
    scol_ss, scol_rs, srow_ss, srow_rs, srow8_ss, srow8_rs,
):
    r = lax.axis_index("row")
    c = lax.axis_index("col")
    up, down = lax.rem(r + NR - 1, NR), lax.rem(r + 1, NR)
    left, right = lax.rem(c + NCOL - 1, NCOL), lax.rem(c + 1, NCOL)

    def local(src, dst, k):
        cp = pltpu.make_async_copy(src, dst, loc.at[k])
        cp.start()
        return cp

    def remote(src, dst, ss, rs_, dev):
        return pltpu.make_async_remote_copy(
            src_ref=src, dst_ref=dst, send_sem=ss, recv_sem=rs_, device_id=dev, device_id_type=MESH
        )

    in_panel = local(panel, panel_v, 0)
    in_gauge = [local(inflow, inflow_v, 1), local(gtile, gtile_v, 2), local(gcell, gcell_v, 3)]
    in_tile = [
        local(depth, stage.at[0], 4),
        local(flow_e, stage.at[1], 5),
        local(flow_s, stage.at[2], 6),
        local(elev, stage.at[3], 7),
        local(rough, stage.at[4], 8),
        local(wet, wet_v, 9),
    ]
    in_rain = [local(rain.at[f], rain_v.at[f], 10 + f) for f in range(FRAMES)]

    barrier = pltpu.get_barrier_semaphore()
    for o in range(1, NCOL):
        pl.semaphore_signal(barrier, inc=1, device_id=(r, lax.rem(c + o, NCOL)), device_id_type=MESH)
    for o in range(1, NR):
        pl.semaphore_signal(barrier, inc=1, device_id=(lax.rem(r + o, NR), c), device_id_type=MESH)
    pl.semaphore_wait(barrier, NCOL + NR - 2)

    in_panel.wait()
    panel_cp = []
    per_tile = STRIPE // PANEL_ROWS
    for o in range(1, NCOL):
        to = lax.rem(c + o, NCOL)
        rows = pl.ds(mul8(to * per_tile // 8), 8)
        cp = remote(panel_v.at[rows, :], panel_r.at[c], panel_ss.at[o], panel_rs.at[o], (r, to))
        cp.start()
        panel_cp.append(cp)
    panel_r[c] = panel_v[pl.ds(mul8(c * per_tile // 8), 8), :]

    for cp in in_gauge:
        cp.wait()
    g0, g1 = iota((GD, GD), 0), iota((GD, GD), 1)
    eye = g0 == g1
    tile_b = jnp.broadcast_to(gtile_v[...].astype(jnp.float32), (GD, GD))
    tile_row = jnp.sum(jnp.where(eye, tile_b, 0.0), axis=0, keepdims=True)
    same = tile_b == tile_row
    rank_col = jnp.sum(jnp.where(same & (g1 < g0), 1.0, 0.0), axis=1, keepdims=True)
    rank_row = jnp.sum(jnp.where(same & (g0 < g1), 1.0, 0.0), axis=0, keepdims=True)
    tile_r = jnp.floor(tile_row * (1.0 / NCOL))
    tile_c = tile_row - tile_r * NCOL
    slot = (tile_c * NR + tile_r) * CAP + rank_row
    slots = NR * NCOL * CAP
    pick = jnp.where(iota((slots, GD), 0).astype(jnp.float32) == slot, 1.0, 0.0).astype(jnp.bfloat16)
    vals = join3(dot(pick, split3(inflow_v[...])))
    cells = jnp.concatenate([gcell_v[k : k + 1, :] for k in range(GD // LANES)], axis=1).astype(jnp.float32)
    cell_col = jnp.sum(jnp.where(eye, cells, 0.0), axis=1, keepdims=True)
    cell_hi = jnp.floor(cell_col * 0.125)
    cell_lo = cell_col - cell_hi * 8.0
    mine = rank_col == lax.rem(iota((GD, LANES), 1), CAP).astype(jnp.float32)
    cell_x = jnp.concatenate([jnp.where(mine, cell_hi, 0.0), jnp.where(mine, cell_lo, 0.0)], axis=1)
    order = iota((NR * NCOL, GD), 0).astype(jnp.float32) == tile_c * NR + tile_r
    cell_y = dot(jnp.where(order, 1.0, 0.0).astype(jnp.bfloat16), cell_x.astype(jnp.bfloat16))
    cell_t = cell_y[:, :LANES] * 8.0 + cell_y[:, LANES:]
    per = NR * CAP
    for k in range(NCOL):
        ga[k, 8 : 8 + per, :] = vals[k * per : (k + 1) * per]
        ga[k, 8 + per : 16 + per, :] = cell_t[k * NR : (k + 1) * NR]
    ga_cp = []
    for o in range(1, NCOL):
        to = lax.rem(c + o, NCOL)
        cp = remote(
            ga.at[to, pl.ds(8, per + 8)], ga_r.at[c, pl.ds(8, per + 8)], ga_ss.at[o], ga_rs.at[o], (r, to)
        )
        cp.start()
        ga_cp.append(cp)
    ga_r[c, pl.ds(8, per + 8), :] = ga[c, pl.ds(8, per + 8), :]

    for cp in in_tile:
        cp.wait()

    def scale_rows(i, _):
        rows = pl.ds(mul8(i), 8)
        to = pl.ds(mul8(i + BASE // 8), 8)
        for b in range(NB):
            cols = pl.ds(b * LANES, LANES)
            z = stage[3, rows, cols] * SCALE
            X[0, b, to, :] = stage[0, rows, cols] * SCALE + z
            X[1, b, to, :] = stage[1, rows, cols] * QSCALE
            X[2, b, to, :] = stage[2, rows, cols] * QSCALE
            X[3, b, to, :] = z
            n = stage[4, rows, cols]
            X[4, b, to, :] = jnp.where(wet_v[rows, cols] > 0, n, -n)
        return 0

    lax.fori_loop(0, TR // 8, scale_rows, 0)
    top_rows, bottom_rows = pl.ds(BASE, HALO), pl.ds(BASE + TR - HALO, HALO)
    top_halo, bottom_halo = pl.ds(BASE - HALO, HALO), pl.ds(BASE + TR, HALO)
    own = pl.ds(BASE, TR)
    tile = pl.ds(0, NB)

    def pair(ref, cols, ss, rs_):
        cps = [
            remote(ref.at[:, cols, bottom_rows, :], ref.at[:, cols, top_halo, :], ss.at[0], rs_.at[0], (down, c)),
            remote(ref.at[:, cols, top_rows, :], ref.at[:, cols, bottom_halo, :], ss.at[1], rs_.at[1], (up, c)),
        ]
        for cp in cps:
            cp.start()
        return cps

    row_cp = pair(X, tile, row_ss, row_rs)

    lane64 = iota((64, LANES), 1)
    quarter = TR // 4

    def packed(ref, k, block, shift):
        parts = [
            pltpu.roll(ref[k, block, pl.ds(BASE + q * quarter, quarter), :], (32 * q + shift) % LANES, 1)
            for q in range(4)
        ]
        return jnp.where(
            lane64 < 64, jnp.where(lane64 < 32, parts[0], parts[1]), jnp.where(lane64 < 96, parts[2], parts[3])
        )

    def unpacked(from_right, from_left, q):
        a, b = from_right, from_left
        if q:
            a = pltpu.roll(a, LANES - 32 * q, 1)
        if q != 3:
            b = pltpu.roll(b, 96 - 32 * q, 1)
        return jnp.where(lane64 < 64, a, b)

    for k in range(NX):
        pack_l[k] = packed(X, k, 0, 0)
        pack_r[k] = packed(X, k, NB - 1, 32)
    col_cp = [
        remote(pack_l, got_r, col_ss.at[0], col_rs.at[0], (r, left)),
        remote(pack_r, got_l, col_ss.at[1], col_rs.at[1], (r, right)),
    ]
    for cp in col_cp:
        cp.start()

    for cp in panel_cp:
        cp.wait()
    at = lax.rem(c * per_tile, 8)
    upper = iota((STRIPE, LANES), 0) < PANEL_ROWS

    def choose(f, to):
        first = panel_r[to, pl.ds(at, 1), :]
        second = panel_r[to, pl.ds(at + 1, 1), :]
        res = []
        for b in range(NB):
            cols = pl.ds(pl.multiple_of(to * (NB * LANES) + b * LANES, LANES), LANES)
            p = jnp.where(
                upper,
                jnp.broadcast_to(first[:, b : b + 1], (STRIPE, LANES)),
                jnp.broadcast_to(second[:, b : b + 1], (STRIPE, LANES)),
            )
            x = rain_v[f, 0, :, cols].astype(jnp.float32)
            for s in range(1, SOURCES):
                x = jnp.where(p == s, rain_v[f, s, :, cols].astype(jnp.float32), x)
            res.append(x.astype(jnp.bfloat16))
        return res

    my_rows = pl.ds(pl.multiple_of(c * STRIPE, STRIPE), STRIPE)

    def rain_copy(f, o):
        to = lax.rem(c + o, NCOL)
        return remote(rs.at[f, to], rx.at[f, :, my_rows, :], rain_ss.at[f, o], rain_rs.at[f, o], (r, to))

    def send_rain(f):
        def one(o, _):
            to = lax.rem(c + o, NCOL)
            for b, x in enumerate(choose(f, to)):
                rs[f, to, b] = x
            rain_copy(f, o).start()
            return 0

        lax.fori_loop(1, NCOL, one, 0)
        for b, x in enumerate(choose(f, c)):
            rx[f, b, my_rows, :] = x

    in_rain[0].wait()
    send_rain(0)

    for cp in ga_cp:
        cp.wait()
    half = iota((8, LANES), 0) < CAP
    lane8 = iota((8, LANES), 1)
    cc = jnp.zeros((8, LANES), jnp.float32)
    for k in range(NCOL):
        cc = cc + jnp.where(lane8 // CAP == k, ga_r[k, 8 + per : 16 + per, :], 0.0)
    for q in range(NR):
        for p in range(NCOL // 2):
            lo8 = ga_r[2 * p, pl.ds(8 + CAP * q, 8), :]
            hi8 = ga_r[2 * p + 1, pl.ds(8 - CAP + CAP * q, 8), :]
            gb[q, p * 8 : p * 8 + 8, :] = jnp.where(half, lo8, hi8)
        gb[q, NCOL * CAP : NCOL * CAP + 8, :] = jnp.broadcast_to(cc[q : q + 1], (8, LANES))
    gb_cp = []
    for o in range(1, NR):
        to = lax.rem(r + o, NR)
        cp = remote(gb.at[to], gb_r.at[r], gb_ss.at[o], gb_rs.at[o], (to, c))
        cp.start()
        gb_cp.append(cp)
    gb_r[r] = gb[r]

    for cp in col_cp:
        cp.wait()
    inside = ((lane64 < 32) & (c < NCOL - 1)) | ((lane64 >= 96) & (c > 0))
    for k in range(NX):
        for q in range(4):
            x = unpacked(got_r[k], got_l[k], q)
            if k == 4:
                x = jnp.where(inside, x, 0.0)
            X[k, NB, pl.ds(BASE + q * quarter, quarter), :] = x
    row8_cp = pair(X, pl.ds(NB, 1), row8_ss, row8_rs)

    in_rain[1].wait()
    send_rain(1)

    for cp in gb_cp:
        cp.wait()
    pieces = []
    for k in range(0, NR, 2):
        a = gb_r[k, NCOL * CAP : NCOL * CAP + 1, :]
        b = pltpu.roll(gb_r[k + 1, NCOL * CAP : NCOL * CAP + 8, :], 64, 1)[0:1]
        pieces.append(jnp.where(iota((1, LANES), 1) < 64, a, b))
    cell_row = jnp.concatenate(pieces, axis=1)
    got = split3(jnp.concatenate([gb_r[k, 0 : NCOL * CAP, :] for k in range(NR)], axis=0))

    def fill(b, _):
        at_cell = (iota((TR, slots), 0) * NB + b).astype(jnp.float32)
        hot = jnp.where(at_cell == cell_row, 1.0, 0.0).astype(jnp.bfloat16)
        SG[b] = join3(dot(hot, got))
        return 0

    lax.fori_loop(0, NB, fill, 0)

    for cp in row_cp + row8_cp:
        cp.wait()
    zero = jnp.zeros((8, LANES), jnp.float32)
    for k in range(NX):
        for b in range(NB + 1):
            X[k, b, 0:8, :] = zero
            X[k, b, RP - 8 : RP, :] = zero

    @pl.when(r == 0)
    def _():
        for b in range(NB + 1):
            X[4, b, top_halo, :] = jnp.zeros((HALO, LANES), jnp.float32)

    @pl.when(r == NR - 1)
    def _():
        for b in range(NB + 1):
            X[4, b, bottom_halo, :] = jnp.zeros((HALO, LANES), jnp.float32)

    last = lane8 == LANES - 1
    first = lane8 == 0

    def eastward(xs):
        ro = [pltpu.roll(x, LANES - 1, 1) for x in xs]
        return [jnp.where(last, ro[(b + 1) % (NB + 1)], ro[b]) for b in range(NB + 1)]

    def prepare(i, _):
        rows = pl.ds(mul8(i), 8)
        south = pl.ds(mul8(i) + 1, 8)
        zs = [X[3, b, rows, :] for b in range(NB + 1)]
        ns = [X[4, b, rows, :] for b in range(NB + 1)]
        ze, ne = eastward(zs), eastward(ns)
        en = eastward([X[0, b, rows, :] for b in range(NB + 1)])
        for b in range(NB + 1):
            EN[b, rows, :] = en[b]
            for zn, nn, Z, F, B in (
                (ze[b], ne[b], ZE, FE, BE),
                (X[3, b, south, :], X[4, b, south, :], ZS, FS, BS),
            ):
                Z[b, rows, :] = jnp.maximum(zs[b], zn)
                n = jnp.abs(ns[b]) + jnp.abs(nn)
                F[b, rows, :] = FRIC * (n * n)
                B[b, rows, :] = jnp.where(jnp.minimum(ns[b], nn) > 0.0, 1.0, jnp.inf)
        return 0

    lax.fori_loop(0, RP // 8 - 1, prepare, 0)

    def scol(f):
        return [
            remote(spack_l.at[f], sgot_r.at[f], scol_ss.at[f, 0], scol_rs.at[f, 0], (r, left)),
            remote(spack_r.at[f], sgot_l.at[f], scol_ss.at[f, 1], scol_rs.at[f, 1], (r, right)),
        ]

    def srow(f, cols, ss, rs_):
        return [
            remote(S.at[f, cols, bottom_rows, :], S.at[f, cols, top_halo, :], ss.at[f, 0], rs_.at[f, 0], (down, c)),
            remote(S.at[f, cols, top_rows, :], S.at[f, cols, bottom_halo, :], ss.at[f, 1], rs_.at[f, 1], (up, c)),
        ]

    def sources1(f):
        def wait_rain(o, _):
            rain_copy(f, o).wait()
            return 0

        lax.fori_loop(1, NCOL, wait_rain, 0)

        def add(i, _):
            rows = pl.ds(pl.multiple_of(i * 16, 16), 16)
            for b in range(NB):
                S[f, b, pl.ds(pl.multiple_of(i * 16 + BASE, 16), 16), :] = SCALE * (
                    rx[f, b, rows, :].astype(jnp.float32) + SG[b, rows, :]
                )
            return 0

        lax.fori_loop(0, TR // 16, add, 0)
        spack_l[f] = packed(S, f, 0, 0)
        spack_r[f] = packed(S, f, NB - 1, 32)
        for cp in scol(f) + srow(f, tile, srow_ss, srow_rs):
            cp.start()

    def sources2(f):
        for cp in scol(f):
            cp.wait()
        for q in range(4):
            S[f, NB, pl.ds(BASE + q * quarter, quarter), :] = unpacked(sgot_r[f], sgot_l[f], q)
        for cp in srow(f, pl.ds(NB, 1), srow8_ss, srow8_rs):
            cp.start()

    def sources3(f):
        for cp in srow(f, tile, srow_ss, srow_rs) + srow(f, pl.ds(NB, 1), srow8_ss, srow8_rs):
            cp.wait()
        for b in range(NB + 1):
            S[f, b, 0:8, :] = zero
            S[f, b, RP - 8 : RP, :] = zero

    sources1(0)
    sources2(0)
    sources3(0)

    def faces(rho):
        rows = pl.ds(rho, 8)
        for b in range(NB + 1):
            eta = X[0, b, rows, :]
            X[1, b, rows, :] = face(eta, EN[b, rows, :], X[1, b, rows, :], ZE[b, rows, :], FE[b, rows, :], BE[b, rows, :])
            X[2, b, rows, :] = face(
                eta, X[0, b, pl.ds(rho + 1, 8), :], X[2, b, rows, :], ZS[b, rows, :], FS[b, rows, :], BS[b, rows, :]
            )

    def update(f, rho):
        rows = pl.ds(rho, 8)
        qe = [X[1, b, rows, :] for b in range(NB + 1)]
        ro = [pltpu.roll(x, 1, 1) for x in qe]
        eta = []
        for b in range(NB + 1):
            west = jnp.where(first, ro[(b - 1) % (NB + 1)], ro[b])
            x = (
                X[0, b, rows, :]
                + ((west - qe[b]) + (X[2, b, pl.ds(rho - 1, 8), :] - X[2, b, rows, :]))
                + S[f, b, rows, :]
            )
            eta.append(x)
            X[0, b, rows, :] = x
        for b, x in enumerate(eastward(eta)):
            EN[b, rows, :] = x

    def step(t, _):
        @pl.when(t == 2)
        def _():
            sources1(1)

        @pl.when(t == 5)
        def _():
            sources2(1)

        @pl.when(t == STEPS // FRAMES)
        def _():
            sources3(1)

        f = t * FRAMES // STEPS
        m = STEPS - 1 - t
        lo = BASE // 8 - (m // 8 + 1)
        hi = (BASE + TR) // 8 + (m + 7) // 8
        hi = hi + lax.rem(hi - lo, 2)
        big = (hi - lo) // 6

        def six(i, _):
            for k in range(6):
                rho = mul8(lo + i * 6 + k)
                faces(rho)
                update(f, rho)
            return 0

        def two(i, _):
            for k in range(2):
                rho = mul8(lo + big * 6 + i * 2 + k)
                faces(rho)
                update(f, rho)
            return 0

        lax.fori_loop(0, big, six, 0)
        lax.fori_loop(0, (hi - lo - big * 6) // 2, two, 0)
        return 0

    lax.fori_loop(0, STEPS, step, 0)

    def finish(i, _):
        rows = pl.ds(mul8(i), 8)
        at_ = pl.ds(mul8(i + BASE // 8), 8)
        for b in range(NB):
            cols = pl.ds(b * LANES, LANES)
            outs[0, rows, cols] = (X[0, b, at_, :] - X[3, b, at_, :]) * (1.0 / SCALE)
            outs[1, rows, cols] = X[1, b, at_, :] * (1.0 / QSCALE)
            outs[2, rows, cols] = X[2, b, at_, :] * (1.0 / QSCALE)
        return 0

    lax.fori_loop(0, TR // 8, finish, 0)
    done = [local(outs.at[0], out_h, 12), local(outs.at[1], out_e, 13), local(outs.at[2], out_s, 14)]
    for cp in done:
        cp.wait()


def body(depth, flow_e, flow_s, elev, rough, wet, rain, panel, inflow, gtile, gcell):
    f32, bf16, i32 = jnp.float32, jnp.bfloat16, jnp.int32
    dma = pltpu.SemaphoreType.DMA
    rows, cols = depth.shape
    per = NR * CAP
    ext = pltpu.VMEM((NB + 1, RP, LANES), f32)
    scratch = [
        pltpu.VMEM((NX, rows, cols), f32),
        pltpu.VMEM((rows, cols), i32),
        pltpu.VMEM(rain.shape, bf16),
        pltpu.VMEM(panel.shape, i32),
        pltpu.VMEM(inflow.shape, f32),
        pltpu.VMEM(gtile.shape, i32),
        pltpu.VMEM((GD // LANES, LANES), i32),
        pltpu.VMEM((NX, NB + 1, RP, LANES), f32),
        ext, ext, ext, ext, ext, ext, ext,
        pltpu.VMEM((FRAMES, NB + 1, RP, LANES), f32),
        pltpu.VMEM((NB, rows, LANES), f32),
        pltpu.VMEM((NCOL, 8, panel.shape[1]), i32),
        pltpu.VMEM((NCOL, per + 16, LANES), f32),
        pltpu.VMEM((NCOL, per + 16, LANES), f32),
        pltpu.VMEM((NR, NCOL * CAP + 8, LANES), f32),
        pltpu.VMEM((NR, NCOL * CAP + 8, LANES), f32),
        pltpu.VMEM((FRAMES, NCOL, NB, STRIPE, LANES), bf16),
        pltpu.VMEM((FRAMES, NB, rows, LANES), bf16),
        *([pltpu.VMEM((NX, rows // 4, LANES), f32)] * 4),
        *([pltpu.VMEM((FRAMES, rows // 4, LANES), f32)] * 4),
        pltpu.VMEM((3, rows, cols), f32),
        dma((15,)),
        dma((NCOL,)), dma((NCOL,)),
        dma((NCOL,)), dma((NCOL,)),
        dma((NR,)), dma((NR,)),
        dma((FRAMES, NCOL)), dma((FRAMES, NCOL)),
        dma((2,)), dma((2,)),
        dma((2,)), dma((2,)),
        dma((2,)), dma((2,)),
        dma((FRAMES, 2)), dma((FRAMES, 2)),
        dma((FRAMES, 2)), dma((FRAMES, 2)),
        dma((FRAMES, 2)), dma((FRAMES, 2)),
    ]
    out = jax.ShapeDtypeStruct(depth.shape, f32)
    hbm = pl.BlockSpec(memory_space=pl.ANY)
    return pl.pallas_call(
        kernel,
        out_shape=(out, out, out),
        in_specs=[hbm] * 11,
        out_specs=(hbm, hbm, hbm),
        scratch_shapes=scratch,
        compiler_params=pltpu.CompilerParams(
            collective_id=0, has_side_effects=True, vmem_limit_bytes=60 * 1024 * 1024
        ),
        name="inundation",
    )(depth, flow_e, flow_s, elev, rough, wet, rain, panel, inflow, gtile, gcell.reshape(GD // LANES, LANES))


def solution(mesh):
    placed = (
        P("row", "col"),
        P("row", "col"),
        P("row", "col"),
        P("row", "col"),
        P("row", "col"),
        P("row", "col"),
        P(None, None, ("row", "col"), None),
        P("row", "col"),
        P(("row", "col"), None),
        P(("row", "col"), None),
        P(("row", "col")),
    )
    return jax.shard_map(
        body,
        mesh=mesh,
        in_specs=placed,
        out_specs=(P("row", "col"), P("row", "col"), P("row", "col")),
        check_vma=False,
    )
```

time: 943 us -> 122 us (0.13)
  the two profiles are of different devices: /device:TPU:38 before, /device:TPU:32 now
where the time goes in v1:
time: 122 us
  Pallas kernels  113 us (93%)
  local copies, waits for them, and re-layouts  8.51 us (7%)
    pallas_call x1, Pallas kernels, body(): pl.pallas_call(kernel, out_shape=(out, out, out), in_specs=[hbm] * 11, ou...  113 us
    unnamed x7, local copies, waits for them, and re-layouts  8.51 us

profile of v1, /device:TPU:32, one launch (start us, length us, event | category | flops | bytes accessed | tf_op | source)
XLA Modules:
  0.0 121.9 jit_solution(4420589711664080454)
XLA Ops:
  0.6 1.4 %copy.14.panel = s32[32,8]{1,0:T(8,128)} copy(s32[32,8]{0,1:T(8,128)} %param.18) | data formatting | bytes 2048 | tf_op args[7]
  2.0 1.5 %copy.15.gtile = s32[256,1]{1,0:T(8,128)} copy(s32[256,1]{0,1:T(1,128)} %param.20) | data formatting | bytes 2048 | tf_op args[9]
  3.5 112.7 %inundation.1 = (f32[256,1024]{1,0:T(8,128)}, f32[256,1024]{1,0:T(8,128)}, f32[256,1024]{1,0:T(8,128)}) custom-call(f32[256,1024]{1,0:T(8,128)} %depth.1, f32[256,1024]{1,0:T(8,128)} %flow_e.1, f32[256,1024]{1,0:T(8,128)} %flow_s.1, f32[256,1024]{1,0:T(8,128)} %elev.1, f32[256,1024]{1,0:T(8,128)} %rough.1, s32[256,1024]{1,0:T(8,128)} %wet.1, ...), custom_call_target="tpu_custom_call" | custom-call | tf_op jit(solution)/shard_map/inundation/pallas_call | solution.py:544
  116.2 0.0 copy-start
  116.2 2.4 %copy.19 = f32[256,1024]{1,0:T(8,128)} copy(f32[256,1024]{1,0:T(8,128)} %get-tuple-element.6) | data formatting | bytes 2097152
  118.6 2.3 %copy.20 = f32[256,1024]{1,0:T(8,128)} copy(f32[256,1024]{1,0:T(8,128)} %get-tuple-element.7) | data formatting | bytes 2097152
  120.9 0.0 copy-done
  120.9 1.0 copy.21
Async XLA Ops:
  116.2 4.7 %copy-start = (f32[256,1024]{1,0:T(8,128)S(1)}, f32[256,1024]{1,0:T(8,128)}, u32[]{:S(2)}) copy-start(f32[256,1024]{1,0:T(8,128)} %get-tuple-element.8) | copy-start | bytes 3145732

commit v2 on v1

v2 whole, which is shorter than its diff:
```python
import functools

import jax
import jax.numpy as jnp
from jax import lax
from jax.experimental import pallas as pl
from jax.experimental.pallas import tpu as pltpu
from jax.sharding import PartitionSpec as P

STEPS = 20
FRAMES = 2
SOURCES = 3
PANEL_ROWS = 8
LANES = 128
CAP = 4
NR = 8
NCOL = 16
TR = 256
NB = 8
HALO = 8
BASE = 16
RP = BASE + TR + 16
SPAN = 7
MID = tuple(range(SPAN, STEPS, SPAN))
STRIPE = TR // NCOL
GD = 256
NX = 5

GRAVITY = 9.81
DT = 5.0
DX = 90.0
RATIO = DT / DX
SCALE = RATIO * GRAVITY * DT / DX
QSCALE = SCALE * RATIO
FLOOR = 0.1 * SCALE
FRIC = GRAVITY * DT * 0.25 * SCALE ** (7.0 / 3.0) / QSCALE
VMEM_LIMIT = 60 * 1024 * 1024
PART = 128
MESH = pl.DeviceIdType.MESH


def split3(x):
    hi = x.astype(jnp.bfloat16)
    rest = x - hi.astype(jnp.float32)
    mid = rest.astype(jnp.bfloat16)
    low = (rest - mid.astype(jnp.float32)).astype(jnp.bfloat16)
    return jnp.concatenate([hi, mid, low], axis=1)


def join3(x):
    return (x[:, :LANES] + x[:, LANES : 2 * LANES]) + x[:, 2 * LANES :]


def dot(a, b):
    return lax.dot_general(a, b, (((1,), (0,)), ((), ())), preferred_element_type=jnp.float32)


def iota(shape, axis):
    return lax.broadcasted_iota(jnp.int32, shape, axis)


def face(eta, nxt, q, zmax, fric, base):
    hf = jnp.maximum(jnp.maximum(eta, nxt) - zmax, FLOOR)
    drv = q - hf * (nxt - eta)
    pw = jnp.exp2(jnp.log2(hf) * (-7.0 / 3.0))
    return drv * (1.0 / (base + jnp.abs(q) * fric * pw))


def mul8(x):
    return pl.multiple_of(x * 8, 8)


def kernel(
    depth, flow_e, flow_s, elev, rough, wet, rain, panel, inflow, gtile, gcell,
    out,
    stage, wet_v, rain_v, panel_v, inflow_v, gtile_v, gcell_v,
    X, ZE, ZS, FE, FS, BE, BS, EN, S, SG,
    panel_r, ga, ga_r, gb, gb_r, rs, rx, pack_l, pack_r, got_l, got_r, spack_l, spack_r, sgot_l, sgot_r, corner, scorner, mid_out, mid_in,
    loc, panel_ss, panel_rs, ga_ss, ga_rs, gb_ss, gb_rs, rain_ss, rain_rs,
    halo_ss, halo_rs, shalo_ss, shalo_rs, mid_ss, mid_rs,
):
    r = lax.axis_index("row")
    c = lax.axis_index("col")
    up, down = lax.rem(r + NR - 1, NR), lax.rem(r + 1, NR)
    left, right = lax.rem(c + NCOL - 1, NCOL), lax.rem(c + 1, NCOL)

    def local(src, dst, k):
        cp = pltpu.make_async_copy(src, dst, loc.at[k])
        cp.start()
        return cp

    def remote(src, dst, ss, rs_, dev):
        return pltpu.make_async_remote_copy(
            src_ref=src, dst_ref=dst, send_sem=ss, recv_sem=rs_, device_id=dev, device_id_type=MESH
        )

    in_panel = local(panel, panel_v, 0)
    in_gauge = [local(inflow, inflow_v, 1), local(gtile, gtile_v, 2), local(gcell, gcell_v, 3)]
    in_tile = [
        local(depth, stage.at[0], 4),
        local(flow_e, stage.at[1], 5),
        local(flow_s, stage.at[2], 6),
        local(elev, stage.at[3], 7),
        local(rough, stage.at[4], 8),
        local(wet, wet_v, 9),
    ]
    in_rain = [local(rain.at[f], rain_v.at[f], 10 + f) for f in range(FRAMES)]

    barrier = pltpu.get_barrier_semaphore()
    partners = [(r, lax.rem(c + o, NCOL)) for o in range(1, NCOL)]
    partners += [(lax.rem(r + o, NR), c) for o in range(1, NR)]
    partners += [(v, h) for v in (up, down) for h in (left, right)]
    for dev in partners:
        pl.semaphore_signal(barrier, inc=1, device_id=dev, device_id_type=MESH)

    for cp in in_gauge:
        cp.wait()
    g0, g1 = iota((GD, GD), 0), iota((GD, GD), 1)
    eye = g0 == g1

    def as_row(ref):
        return jnp.concatenate([ref[k : k + 1, :] for k in range(GD // LANES)], axis=1).astype(jnp.float32)

    def as_col(row):
        return jnp.sum(jnp.where(eye, row, 0.0), axis=1, keepdims=True)

    tile_row = as_row(gtile_v)
    same = as_col(tile_row) == tile_row
    rank_col = jnp.sum(jnp.where(same & (g1 < g0), 1.0, 0.0), axis=1, keepdims=True)
    rank_row = jnp.sum(jnp.where(same & (g0 < g1), 1.0, 0.0), axis=0, keepdims=True)
    tile_r = jnp.floor(tile_row * (1.0 / NCOL))
    tile_c = tile_row - tile_r * NCOL
    place = tile_c * NR + tile_r
    slot = place * CAP + rank_row
    slots = NR * NCOL * CAP
    pick = jnp.where(iota((slots, GD), 0).astype(jnp.float32) == slot, 1.0, 0.0).astype(jnp.bfloat16)
    vals = join3(dot(pick, split3(inflow_v[...])))
    cell_col = as_col(as_row(gcell_v))
    cell_hi = jnp.floor(cell_col * 0.125)
    cell_lo = cell_col - cell_hi * 8.0
    mine = rank_col == lax.rem(iota((GD, LANES), 1), CAP).astype(jnp.float32)
    cell_x = jnp.concatenate([jnp.where(mine, cell_hi, 0.0), jnp.where(mine, cell_lo, 0.0)], axis=1)
    order = iota((NR * NCOL, GD), 0).astype(jnp.float32) == place
    cell_y = dot(jnp.where(order, 1.0, 0.0).astype(jnp.bfloat16), cell_x.astype(jnp.bfloat16))
    cell_t = cell_y[:, :LANES] * 8.0 + cell_y[:, LANES:]
    per = NR * CAP
    for k in range(NCOL):
        ga[k, 8 : 8 + per, :] = vals[k * per : (k + 1) * per]
        ga[k, 8 + per : 16 + per, :] = cell_t[k * NR : (k + 1) * NR]

    for cp in in_tile:
        cp.wait()

    def scale_rows(i, _):
        rows = pl.ds(mul8(i), 8)
        to = pl.ds(mul8(i + BASE // 8), 8)
        for b in range(NB):
            cols = pl.ds(b * LANES, LANES)
            z = stage[3, rows, cols] * SCALE
            X[0, b, to, :] = stage[0, rows, cols] * SCALE + z
            X[1, b, to, :] = stage[1, rows, cols] * QSCALE
            X[2, b, to, :] = stage[2, rows, cols] * QSCALE
            X[3, b, to, :] = z
            n = stage[4, rows, cols]
            X[4, b, to, :] = jnp.where(wet_v[rows, cols] > 0, n, -n)
        return 0

    lax.fori_loop(0, TR // 8, scale_rows, 0)
    top_rows, bottom_rows = pl.ds(BASE, HALO), pl.ds(BASE + TR - HALO, HALO)
    top_halo, bottom_halo = pl.ds(BASE - HALO, HALO), pl.ds(BASE + TR, HALO)
    tile = pl.ds(0, NB)
    quarter = TR // 4
    lane_h = iota((quarter, LANES), 1)
    ends = pl.ds(0, HALO), pl.ds(quarter - HALO, HALO)

    def packed(ref, k, block, shift):
        parts = [
            pltpu.roll(ref[k, block, pl.ds(BASE + q * quarter, quarter), :], (32 * q + shift) % LANES, 1)
            for q in range(4)
        ]
        return jnp.where(
            lane_h < 64, jnp.where(lane_h < 32, parts[0], parts[1]), jnp.where(lane_h < 96, parts[2], parts[3])
        )

    def unpacked(from_right, from_left, q):
        a, b = from_right, from_left
        if q:
            a = pltpu.roll(a, LANES - 32 * q, 1)
        if q != 3:
            b = pltpu.roll(b, 96 - 32 * q, 1)
        return jnp.where(iota(a.shape, 1) < 64, a, b)

    for k in range(NX):
        pack_l[k] = packed(X, k, 0, 0)
        pack_r[k] = packed(X, k, NB - 1, 32)

    in_panel.wait()
    pl.semaphore_wait(barrier, len(partners))

    panel_cp, ga_cp = [], []
    for o in range(1, NCOL):
        to = lax.rem(c + o, NCOL)
        cp = remote(panel_v, panel_r.at[c], panel_ss.at[o], panel_rs.at[o], (r, to))
        cp.start()
        panel_cp.append(cp)
    hop = pl.ds(8, per + 8)
    for o in range(1, NCOL):
        to = lax.rem(c + o, NCOL)
        cp = remote(ga.at[to, hop], ga_r.at[c, hop], ga_ss.at[o], ga_rs.at[o], (r, to))
        cp.start()
        ga_cp.append(cp)
    panel_r[c] = panel_v[...]
    ga_r[c, hop, :] = ga[c, hop, :]

    has_up, has_down, has_left, has_right = r > 0, r < NR - 1, c > 0, c < NCOL - 1

    def row_copies(ref, ss, rs_):
        return [
            (remote(ref.at[:, tile, bottom_rows, :], ref.at[:, tile, top_halo, :], ss(0), rs_(0), (down, c)),
             has_down, has_up),
            (remote(ref.at[:, tile, top_rows, :], ref.at[:, tile, bottom_halo, :], ss(1), rs_(1), (up, c)),
             has_up, has_down),
        ]

    def col_copies(pl_, pr_, gl, gr, cn, ss, rs_):
        return [
            (remote(pl_, gr, ss(2), rs_(2), (r, left)), has_left, has_right),
            (remote(pr_, gl, ss(3), rs_(3), (r, right)), has_right, has_left),
            (remote(pl_.at[:, ends[1], :], cn.at[0], ss(4), rs_(4), (down, left)),
             has_down & has_left, has_up & has_right),
            (remote(pr_.at[:, ends[1], :], cn.at[1], ss(5), rs_(5), (down, right)),
             has_down & has_right, has_up & has_left),
            (remote(pl_.at[:, ends[0], :], cn.at[2], ss(6), rs_(6), (up, left)),
             has_up & has_left, has_down & has_right),
            (remote(pr_.at[:, ends[0], :], cn.at[3], ss(7), rs_(7), (up, right)),
             has_up & has_right, has_down & has_left),
        ]

    def start_all(copies):
        for cp, sends, _ in copies:
            pl.when(sends)(cp.start)

    def wait_sent(copies):
        for cp, sends, _ in copies:
            pl.when(sends)(cp.wait_send)

    def wait_got(copies):
        for cp, _, gets in copies:
            pl.when(gets)(cp.wait_recv)

    def wait_all(copies):
        wait_sent(copies)
        wait_got(copies)

    def beside(x):
        lane = iota(x.shape, 1)
        return jnp.where(((lane < 32) & has_right) | ((lane >= 96) & has_left), x, 0.0)

    def clear_border(ref, k):
        @pl.when(r == 0)
        def _():
            for b in range(NB + 1):
                ref[k, b, top_halo, :] = jnp.zeros((HALO, LANES), jnp.float32)

        @pl.when(r == NR - 1)
        def _():
            for b in range(NB + 1):
                ref[k, b, bottom_halo, :] = jnp.zeros((HALO, LANES), jnp.float32)

    sem = lambda ref: (lambda k: ref.at[k])
    row_cp = row_copies(X, sem(halo_ss), sem(halo_rs))
    col_cp = col_copies(pack_l, pack_r, got_l, got_r, corner, sem(halo_ss), sem(halo_rs))
    start_all(col_cp + row_cp)

    for cp in panel_cp:
        cp.wait()
    at = c * (STRIPE // PANEL_ROWS)
    upper = iota((STRIPE, LANES), 0) < PANEL_ROWS

    def choose(f, to):
        x = panel_r[to].astype(jnp.float32)
        lane_p = iota(x.shape, 1)
        first = jnp.sum(jnp.where(lane_p == at, x, 0.0), axis=1, keepdims=True)
        second = jnp.sum(jnp.where(lane_p == at + 1, x, 0.0), axis=1, keepdims=True)
        res = []
        for b in range(NB):
            cols = pl.ds(pl.multiple_of(to * (NB * LANES) + b * LANES, LANES), LANES)
            p = jnp.where(
                upper,
                jnp.broadcast_to(first[b : b + 1], (STRIPE, LANES)),
                jnp.broadcast_to(second[b : b + 1], (STRIPE, LANES)),
            )
            x = rain_v[f, 0, :, cols].astype(jnp.float32)
            for s in range(1, SOURCES):
                x = jnp.where(p == s, rain_v[f, s, :, cols].astype(jnp.float32), x)
            res.append(x.astype(jnp.bfloat16))
        return res

    my_rows = pl.ds(pl.multiple_of(c * STRIPE, STRIPE), STRIPE)

    def rain_copy(f, o):
        to = lax.rem(c + o, NCOL)
        return remote(rs.at[f, to], rx.at[f, :, my_rows, :], rain_ss.at[f, o], rain_rs.at[f, o], (r, to))

    def choose_rain(f, send):
        in_rain[f].wait()

        def one(o, _):
            to = lax.rem(c + o, NCOL)
            for b, x in enumerate(choose(f, to)):
                rs[f, to, b] = x
            if send:
                rain_copy(f, o).start()
            return 0

        lax.fori_loop(1, NCOL, one, 0)
        for b, x in enumerate(choose(f, c)):
            rx[f, b, my_rows, :] = x

    choose_rain(0, True)

    for cp in ga_cp:
        cp.wait()
    half = iota((8, LANES), 0) < CAP
    lane8 = iota((8, LANES), 1)
    cc = jnp.zeros((8, LANES), jnp.float32)
    for k in range(NCOL):
        cc = cc + jnp.where(lane8 // CAP == k, ga_r[k, 8 + per : 16 + per, :], 0.0)
    for q in range(NR):
        for p in range(NCOL // 2):
            lo8 = ga_r[2 * p, pl.ds(8 + CAP * q, 8), :]
            hi8 = ga_r[2 * p + 1, pl.ds(8 - CAP + CAP * q, 8), :]
            gb[q, p * 8 : p * 8 + 8, :] = jnp.where(half, lo8, hi8)
        gb[q, NCOL * CAP : NCOL * CAP + 8, :] = jnp.broadcast_to(cc[q : q + 1], (8, LANES))
    gb_cp = []
    for o in range(1, NR):
        to = lax.rem(r + o, NR)
        cp = remote(gb.at[to], gb_r.at[r], gb_ss.at[o], gb_rs.at[o], (to, c))
        cp.start()
        gb_cp.append(cp)
    gb_r[r] = gb[r]

    wait_all(col_cp)

    zero = jnp.zeros((8, LANES), jnp.float32)
    for k in range(NX):
        for q in range(4):
            X[k, NB, pl.ds(BASE + q * quarter, quarter), :] = beside(unpacked(got_r[k], got_l[k], q))
        for b in range(NB + 1):
            X[k, b, 0:8, :] = zero
            X[k, b, RP - 8 : RP, :] = zero

    last = lane8 == LANES - 1
    first = lane8 == 0

    def eastward(xs):
        ro = [pltpu.roll(x, LANES - 1, 1) for x in xs]
        return [jnp.where(last, ro[(b + 1) % (NB + 1)], ro[b]) for b in range(NB + 1)]

    def prepare(i):
        rows = pl.ds(mul8(i), 8)
        south = pl.ds(mul8(i) + 1, 8)
        zs = [X[3, b, rows, :] for b in range(NB + 1)]
        ns = [X[4, b, rows, :] for b in range(NB + 1)]
        ze, ne = eastward(zs), eastward(ns)
        en = eastward([X[0, b, rows, :] for b in range(NB + 1)])
        for b in range(NB + 1):
            EN[b, rows, :] = en[b]
            for zn, nn, Z, F, B in (
                (ze[b], ne[b], ZE, FE, BE),
                (X[3, b, south, :], X[4, b, south, :], ZS, FS, BS),
            ):
                Z[b, rows, :] = jnp.maximum(zs[b], zn)
                n = jnp.abs(ns[b]) + jnp.abs(nn)
                F[b, rows, :] = FRIC * (n * n)
                B[b, rows, :] = jnp.where(jnp.minimum(ns[b], nn) > 0.0, 1.0, jnp.inf)

    own_lo, own_hi = BASE // 8, (BASE + TR) // 8

    def prepare_own(i, _):
        prepare(i)
        return 0

    lax.fori_loop(own_lo, own_hi - 1, prepare_own, 0)

    for cp in gb_cp:
        cp.wait()
    pieces = []
    for k in range(0, NR, 2):
        a = gb_r[k, NCOL * CAP : NCOL * CAP + 1, :]
        b = pltpu.roll(gb_r[k + 1, NCOL * CAP : NCOL * CAP + 8, :], 64, 1)[0:1]
        pieces.append(jnp.where(iota((1, LANES), 1) < 64, a, b))
    cell_row = jnp.concatenate(pieces, axis=1)
    got = split3(jnp.concatenate([gb_r[k, 0 : NCOL * CAP, :] for k in range(NR)], axis=0))

    def fill(b, _):
        at_cell = (iota((TR, slots), 0) * NB + b).astype(jnp.float32)
        hot = jnp.where(at_cell == cell_row, 1.0, 0.0).astype(jnp.bfloat16)
        SG[b] = join3(dot(hot, got))
        return 0

    lax.fori_loop(0, NB, fill, 0)

    def source_rows(f):
        frame = pl.ds(f, 1)
        return row_copies(S.at[frame], lambda k: shalo_ss.at[f, k], lambda k: shalo_rs.at[f, k])

    def source_cols(f):
        frame = pl.ds(f, 1)
        return col_copies(
            spack_l.at[frame], spack_r.at[frame], sgot_l.at[frame], sgot_r.at[frame], scorner.at[f],
            lambda k: shalo_ss.at[f, k], lambda k: shalo_rs.at[f, k],
        )

    def sources_out(f):
        def wait_rain(o, _):
            rain_copy(f, o).wait()
            return 0

        lax.fori_loop(1, NCOL, wait_rain, 0)

        def add(i, _):
            rows = pl.ds(pl.multiple_of(i * 16, 16), 16)
            for b in range(NB):
                S[f, b, pl.ds(pl.multiple_of(i * 16 + BASE, 16), 16), :] = SCALE * (
                    rx[f, b, rows, :].astype(jnp.float32) + SG[b, rows, :]
                )
            return 0

        lax.fori_loop(0, TR // 16, add, 0)
        spack_l[f] = packed(S, f, 0, 0)
        spack_r[f] = packed(S, f, NB - 1, 32)
        start_all(source_cols(f) + source_rows(f))
        for b in range(NB + 1):
            S[f, b, 0:8, :] = zero
            S[f, b, RP - 8 : RP, :] = zero

    def sources_in(f):
        wait_all(source_cols(f) + source_rows(f))
        for q in range(4):
            S[f, NB, pl.ds(BASE + q * quarter, quarter), :] = beside(unpacked(sgot_r[f], sgot_l[f], q))
        S[f, NB, top_halo, :] = beside(unpacked(scorner[f, 0, 0], scorner[f, 1, 0], 3))
        S[f, NB, bottom_halo, :] = beside(unpacked(scorner[f, 2, 0], scorner[f, 3, 0], 0))
        clear_border(S, f)

    sources_out(0)

    choose_rain(1, True)

    def halos_in():
        wait_got(row_cp)
        for k in range(NX):
            X[k, NB, top_halo, :] = beside(unpacked(corner[0, k], corner[1, k], 3))
            X[k, NB, bottom_halo, :] = beside(unpacked(corner[2, k], corner[3, k], 0))
            clear_border(X, k)

        def prepare_halo(i, _):
            prepare(jnp.where(i == 0, own_lo - 1, own_hi - 2 + i))
            return 0

        lax.fori_loop(0, 3, prepare_halo, 0)

    def mid_copies(e):
        return [
            (remote(mid_out.at[e, 0], mid_in.at[e, 0], mid_ss.at[e, 0], mid_rs.at[e, 0], (down, c)), has_down, has_up),
            (remote(mid_out.at[e, 1], mid_in.at[e, 1], mid_ss.at[e, 1], mid_rs.at[e, 1], (up, c)), has_up, has_down),
        ]

    def mid_send(e):
        for k in range(3):
            for b in range(NB + 1):
                mid_out[e, 0, k, b] = X[k, b, bottom_rows, :]
                mid_out[e, 1, k, b] = X[k, b, top_rows, :]
        start_all(mid_copies(e))

    def mid_take(e):
        wait_all(mid_copies(e))
        for side, here, has in ((0, top_halo, has_up), (1, bottom_halo, has_down)):

            @pl.when(has)
            def _():
                for k in range(3):
                    for b in range(NB + 1):
                        X[k, b, here, :] = mid_in[e, side, k, b]
                for b, x in enumerate(eastward([mid_in[e, side, 0, b] for b in range(NB + 1)])):
                    EN[b, here, :] = x

    def faces(rho):
        rows = pl.ds(rho, 8)
        for b in range(NB + 1):
            eta = X[0, b, rows, :]
            X[1, b, rows, :] = face(eta, EN[b, rows, :], X[1, b, rows, :], ZE[b, rows, :], FE[b, rows, :], BE[b, rows, :])
            X[2, b, rows, :] = face(
                eta, X[0, b, pl.ds(rho + 1, 8), :], X[2, b, rows, :], ZS[b, rows, :], FS[b, rows, :], BS[b, rows, :]
            )

    def update(f, rho):
        rows = pl.ds(rho, 8)
        qe = [X[1, b, rows, :] for b in range(NB + 1)]
        ro = [pltpu.roll(x, 1, 1) for x in qe]
        eta = []
        for b in range(NB + 1):
            west = jnp.where(first, ro[(b - 1) % (NB + 1)], ro[b])
            x = (
                X[0, b, rows, :]
                + ((west - qe[b]) + (X[2, b, pl.ds(rho - 1, 8), :] - X[2, b, rows, :]))
                + S[f, b, rows, :]
            )
            eta.append(x)
            X[0, b, rows, :] = x
        for b, x in enumerate(eastward(eta)):
            EN[b, rows, :] = x

    def blocks(count, start, do):
        def run(i, _):
            for k in range(count):
                do(mul8(start + i * count + k))
            return 0

        return run

    lo, hi = own_lo - 1, own_hi + 1

    def step(t, _):
        f = t * FRAMES // STEPS

        @pl.when(t == 5)
        def _():
            sources_out(1)

        @pl.when(t == STEPS // FRAMES)
        def _():
            sources_in(1)

        def both(rho):
            faces(rho)
            update(f, rho)

        def only_update(rho):
            update(f, rho)

        def split(arrive):
            lax.fori_loop(0, 6, blocks(5, own_lo, faces), 0)
            arrive()
            for i in (lo, own_hi - 2, own_hi - 1, own_hi):
                faces(i * 8)
            if arrive is first_halos:
                sources_in(0)
            lax.fori_loop(0, 8, blocks(4, lo, only_update), 0)
            for i in (hi - 2, hi - 1):
                update(f, i * 8)

        def boundary_first(e):
            top, bottom = own_lo, own_hi - 1
            for i in (top - 1, top, top + 1, bottom - 1, bottom, bottom + 1):
                faces(i * 8)
            update(f, top * 8)
            update(f, bottom * 8)
            mid_send(e)
            lax.fori_loop(0, 7, blocks(4, top + 2, faces), 0)
            for i in (top - 1, bottom + 1):
                update(f, i * 8)
            lax.fori_loop(0, 7, blocks(4, top + 1, only_update), 0)
            for i in (bottom - 2, bottom - 1):
                update(f, i * 8)

        first_halos = halos_in

        @pl.when(t == 0)
        def _():
            wait_sent(row_cp)
            split(first_halos)

        for e, at_t in enumerate(MID):

            @pl.when(t == at_t)
            def _():
                split(functools.partial(mid_take, e))

        @pl.when((lax.rem(t, SPAN) != 0) & ((lax.rem(t, SPAN) != SPAN - 1) | (t > MID[-1])))
        def _():
            lax.fori_loop(0, 5, blocks(6, lo, both), 0)
            lax.fori_loop(0, 1, blocks(4, lo + 30, both), 0)

        for e, at_t in enumerate(MID):

            @pl.when(t == at_t - 1)
            def _():
                boundary_first(e)

        return 0

    lax.fori_loop(0, STEPS, step, 0)

    def depth_rows(i, _):
        rows = pl.ds(mul8(i), 8)
        for b in range(NB):
            X[0, b, rows, :] = X[0, b, rows, :] - X[3, b, rows, :]
        return 0

    done = [local(X.at[k, tile, pl.ds(BASE, TR), :], out.at[k], 12 + k) for k in (1, 2)]
    lax.fori_loop(own_lo, own_hi, depth_rows, 0)
    done.append(local(X.at[0, tile, pl.ds(BASE, TR), :], out.at[0], 12))
    for cp in done:
        cp.wait()


def finish(x, out_h, out_e, out_s):
    for b in range(NB):
        cols = slice(b * LANES, (b + 1) * LANES)
        out_h[:, cols] = x[0, b] * (1.0 / SCALE)
        out_e[:, cols] = x[1, b] * (1.0 / QSCALE)
        out_s[:, cols] = x[2, b] * (1.0 / QSCALE)


def body(depth, flow_e, flow_s, elev, rough, wet, rain, panel, inflow, gtile, gcell):
    f32, bf16, i32 = jnp.float32, jnp.bfloat16, jnp.int32
    dma = pltpu.SemaphoreType.DMA
    rows, cols = depth.shape
    ext = pltpu.VMEM((NB + 1, RP, LANES), f32)
    scratch = [
        pltpu.VMEM((NX, rows, cols), f32),
        pltpu.VMEM((rows, cols), i32),
        pltpu.VMEM(rain.shape, bf16),
        pltpu.VMEM(panel.shape[::-1], i32),
        pltpu.VMEM(inflow.shape, f32),
        pltpu.VMEM((GD // LANES, LANES), i32),
        pltpu.VMEM((GD // LANES, LANES), i32),
        pltpu.VMEM((NX, NB + 1, RP, LANES), f32),
        ext, ext, ext, ext, ext, ext, ext,
        pltpu.VMEM((FRAMES, NB + 1, RP, LANES), f32),
        pltpu.VMEM((NB, rows, LANES), f32),
        pltpu.VMEM((NCOL, *panel.shape[::-1]), i32),
        pltpu.VMEM((NCOL, NR * CAP + 16, LANES), f32),
        pltpu.VMEM((NCOL, NR * CAP + 16, LANES), f32),
        pltpu.VMEM((NR, NCOL * CAP + 8, LANES), f32),
        pltpu.VMEM((NR, NCOL * CAP + 8, LANES), f32),
        pltpu.VMEM((FRAMES, NCOL, NB, STRIPE, LANES), bf16),
        pltpu.VMEM((FRAMES, NB, rows, LANES), bf16),
        *([pltpu.VMEM((NX, rows // 4, LANES), f32)] * 4),
        *([pltpu.VMEM((FRAMES, rows // 4, LANES), f32)] * 4),
        pltpu.VMEM((4, NX, HALO, LANES), f32),
        pltpu.VMEM((FRAMES, 4, 1, HALO, LANES), f32),
        *([pltpu.VMEM((len(MID), 2, 3, NB + 1, HALO, LANES), f32)] * 2),
        dma((16,)),
        dma((NCOL,)), dma((NCOL,)),
        dma((NCOL,)), dma((NCOL,)),
        dma((NR,)), dma((NR,)),
        dma((FRAMES, NCOL)), dma((FRAMES, NCOL)),
        dma((8,)), dma((8,)),
        dma((FRAMES, 8)), dma((FRAMES, 8)),
        dma((len(MID), 2)), dma((len(MID), 2)),
    ]
    hbm = pl.BlockSpec(memory_space=pl.ANY)
    state = pl.pallas_call(
        kernel,
        out_shape=jax.ShapeDtypeStruct((3, NB, rows, LANES), f32),
        in_specs=[hbm] * 11,
        out_specs=hbm,
        scratch_shapes=scratch,
        compiler_params=pltpu.CompilerParams(
            collective_id=0, has_side_effects=True, vmem_limit_bytes=VMEM_LIMIT
        ),
        name="inundation",
    )(
        depth, flow_e, flow_s, elev, rough, wet, rain, panel.T, inflow,
        gtile.reshape(GD // LANES, LANES), gcell.reshape(GD // LANES, LANES),
    )
    part = PART
    out = jax.ShapeDtypeStruct(depth.shape, f32)
    return pl.pallas_call(
        finish,
        grid=(rows // part,),
        out_shape=(out, out, out),
        in_specs=[pl.BlockSpec((3, NB, part, LANES), lambda i: (0, 0, i, 0))],
        out_specs=[pl.BlockSpec((part, cols), lambda i: (i, 0))] * 3,
        compiler_params=pltpu.CompilerParams(vmem_limit_bytes=VMEM_LIMIT),
        name="unscale",
    )(state)


def solution(mesh):
    placed = (
        P("row", "col"),
        P("row", "col"),
        P("row", "col"),
        P("row", "col"),
        P("row", "col"),
        P("row", "col"),
        P(None, None, ("row", "col"), None),
        P("row", "col"),
        P(("row", "col"), None),
        P(("row", "col"), None),
        P(("row", "col")),
    )
    return jax.shard_map(
        body,
        mesh=mesh,
        in_specs=placed,
        out_specs=(P("row", "col"), P("row", "col"), P("row", "col")),
        check_vma=False,
    )
```

time: 122 us -> 101 us (0.83)
  the two profiles are of different devices: /device:TPU:32 before, /device:TPU:38 now
where the time goes in v2:
time: 101 us
  Pallas kernels  100 us (99%)
    pallas_call x1, Pallas kernels, body(): pl.pallas_call(kernel, out_shape=jax.ShapeDtypeStruct((3, NB, rows, LANES...  96.9 us
    pallas_call x1, Pallas kernels, body(): pl.pallas_call(finish, grid=(rows // part,), out_shape=(out, out, out), i...  3.3 us

profile of v2, /device:TPU:38, one launch (start us, length us, event | category | flops | bytes accessed | tf_op | source)
XLA Modules:
  0.0 100.9 jit_solution(18019006164866339734)
XLA Ops:
  0.6 96.9 %inundation.1.x = f32[3,8,256,128]{3,2,1,0:T(8,128)} custom-call(f32[256,1024]{1,0:T(8,128)} %depth.1, f32[256,1024]{1,0:T(8,128)} %flow_e.1, f32[256,1024]{1,0:T(8,128)} %flow_s.1, f32[256,1024]{1,0:T(8,128)} %elev.1, f32[256,1024]{1,0:T(8,128)} %rough.1, s32[256,1024]{1,0:T(8,128)} %wet.1, bf16[2,3,16,16384]{3,2,1,0:T(8,128)(2,1)} %rain.1, ...), custom_call_target="tpu_custom_call" | custom-call | tf_op jit(solution)/shard_map/inundation/pallas_call | solution.py:655
  97.6 3.3 %unscale.1 = (f32[256,1024]{1,0:T(8,128)}, f32[256,1024]{1,0:T(8,128)}, f32[256,1024]{1,0:T(8,128)}) custom-call(f32[3,8,256,128]{3,2,1,0:T(8,128)} %inundation.1.x), custom_call_target="tpu_custom_call" | custom-call | tf_op jit(solution)/shard_map/unscale/pallas_call | solution.py:671

commit v3 on v2

--- a/solution.py
+++ b/solution.py
@@ -112,6 +112,17 @@
     partners += [(v, h) for v in (up, down) for h in (left, right)]
     for dev in partners:
         pl.semaphore_signal(barrier, inc=1, device_id=dev, device_id_type=MESH)
+
+    in_panel.wait()
+    pl.semaphore_wait(barrier, len(partners))
+
+    panel_cp, ga_cp = [], []
+    for o in range(1, NCOL):
+        to = lax.rem(c + o, NCOL)
+        cp = remote(panel_v, panel_r.at[c], panel_ss.at[o], panel_rs.at[o], (r, to))
+        cp.start()
+        panel_cp.append(cp)
+    panel_r[c] = panel_v[...]
 
     for cp in in_gauge:
         cp.wait()
@@ -148,6 +159,14 @@
         ga[k, 8 : 8 + per, :] = vals[k * per : (k + 1) * per]
         ga[k, 8 + per : 16 + per, :] = cell_t[k * NR : (k + 1) * NR]
 
+    hop = pl.ds(8, per + 8)
+    for o in range(1, NCOL):
+        to = lax.rem(c + o, NCOL)
+        cp = remote(ga.at[to, hop], ga_r.at[c, hop], ga_ss.at[o], ga_rs.at[o], (r, to))
+        cp.start()
+        ga_cp.append(cp)
+    ga_r[c, hop, :] = ga[c, hop, :]
+
     for cp in in_tile:
         cp.wait()
 
@@ -193,24 +212,6 @@
     for k in range(NX):
         pack_l[k] = packed(X, k, 0, 0)
         pack_r[k] = packed(X, k, NB - 1, 32)
-
-    in_panel.wait()
-    pl.semaphore_wait(barrier, len(partners))
-
-    panel_cp, ga_cp = [], []
-    for o in range(1, NCOL):
-        to = lax.rem(c + o, NCOL)
-        cp = remote(panel_v, panel_r.at[c], panel_ss.at[o], panel_rs.at[o], (r, to))
-        cp.start()
-        panel_cp.append(cp)
-    hop = pl.ds(8, per + 8)
-    for o in range(1, NCOL):
-        to = lax.rem(c + o, NCOL)
-        cp = remote(ga.at[to, hop], ga_r.at[c, hop], ga_ss.at[o], ga_rs.at[o], (r, to))
-        cp.start()
-        ga_cp.append(cp)
-    panel_r[c] = panel_v[...]
-    ga_r[c, hop, :] = ga[c, hop, :]
 
     has_up, has_down, has_left, has_right = r > 0, r < NR - 1, c > 0, c < NCOL - 1
 

time: 101 us -> 99.6 us (0.986)
  Pallas kernels: 100 us -> 97.9 us
    pallas_call x1, Pallas kernels: 96.9 us -> 94.6 us  [body(): pl.pallas_call(kernel, out_shape=jax.ShapeDtypeStruct((3, NB, rows, LANES...]
where the time goes in v3:
time: 99.6 us; the launch traced here: 98.6 us
  Pallas kernels  97.9 us (98%)
    pallas_call x1, Pallas kernels, body(): pl.pallas_call(kernel, out_shape=jax.ShapeDtypeStruct((3, NB, rows, LANES...  94.6 us
    pallas_call x1, Pallas kernels, body(): pl.pallas_call(finish, grid=(rows // part,), out_shape=(out, out, out), i...  3.3 us

profile of v3, /device:TPU:38, one launch (start us, length us, event | category | flops | bytes accessed | tf_op | source)
XLA Modules:
  0.0 98.6 jit_solution(11036026048849111293)
XLA Ops:
  0.6 94.6 %inundation.1.x = f32[3,8,256,128]{3,2,1,0:T(8,128)} custom-call(f32[256,1024]{1,0:T(8,128)} %depth.1, f32[256,1024]{1,0:T(8,128)} %flow_e.1, f32[256,1024]{1,0:T(8,128)} %flow_s.1, f32[256,1024]{1,0:T(8,128)} %elev.1, f32[256,1024]{1,0:T(8,128)} %rough.1, s32[256,1024]{1,0:T(8,128)} %wet.1, bf16[2,3,16,16384]{3,2,1,0:T(8,128)(2,1)} %rain.1, ...), custom_call_target="tpu_custom_call" | custom-call | tf_op jit(solution)/shard_map/inundation/pallas_call | solution.py:656
  95.3 3.3 %unscale.1 = (f32[256,1024]{1,0:T(8,128)}, f32[256,1024]{1,0:T(8,128)}, f32[256,1024]{1,0:T(8,128)}) custom-call(f32[3,8,256,128]{3,2,1,0:T(8,128)} %inundation.1.x), custom_call_target="tpu_custom_call" | custom-call | tf_op jit(solution)/shard_map/unscale/pallas_call | solution.py:672
